TPU v7x, 32 devices: a whole 2x2x4 slice. The times are simulated.
32 devices in a mesh: gx: 8 (over y, x, core), gy: 4 (over z).
Axes of the slice: x: 2, y: 2, z: 4, core: 2. Of those that a mesh axis runs over, the one named last changes fastest.
Arguments:
- ocean_depth: float32 [2048, 2048], P('gx', 'gy'), may hold values from 0.5 to 8
- wet_mask: int32 [2048, 2048], P('gx', 'gy'), may hold values 0 or 1
- manning: float32 [2048, 2048], P('gx', 'gy'), may hold values from 0.5 to 5
- fault_slip: float32 [512], P(('gx', 'gy')), may hold values from 0.3 to 1.2
- pattern: float32 [8192, 8, 128], P(('gx', 'gy')), may hold values from -1 to 1
- foot_tile: int32 [8192, 1], P(('gx', 'gy')), may hold values from 0 to 31; in each aligned block of 256 rows (0 to 255, 256 to 511, ...) at most 16 rows name the same one
- foot_block: int32 [8192], P(('gx', 'gy')), may hold values from 0 to 127
- gauge_row: int32 [512], replicated, may hold values from 0 to 2047, as said below
- gauge_col: int32 [512], replicated, may hold values from 0 to 2047, as said below
- observed: float32 [4, 512], replicated, may hold values from -6 to 6
Outputs:
- final_eta: float32 [2048, 2048], P('gx', 'gy')
- readings: float32 [4, 512], replicated
- source_adjoint: float32 [2048, 2048], P('gx', 'gy')
- grad_slip: float32 [512], P(('gx', 'gy'))
Inputs may be any that keep to these rules, and one draw needn't show every extreme that they name: `foot_tile`: the 256 rows of one device name no tile more than 16 times, a bound that some block reaches. Tile t is the one at tile row t // 4 and tile column t % 4. `gauge_row`: gauges 16 * t to 16 * t + 15 lie in tile t, within three cells of one of its edges. `gauge_col`: see gauge_row.
All inputs are finite; a program needn't handle non-finite values. No bound on the sum of `wet_mask` on one device may be relied on, other than what follows from the above.
Results may differ from a plain program's by a relative error of at most 0.0003.
Values sent between devices are 32-bit elements; how exact they have to be, the bound alone decides.
A program may use at most 128 MiB of HBM per device.

v0:
```python
from functools import partial

import jax
import jax.numpy as jnp
from jax import lax
from jax.experimental import pallas as pl
from jax.experimental.pallas import tpu as pltpu
from jax.sharding import PartitionSpec as P

wave_gain = 0.2
mass_gain = 0.2
min_depth = 0.25
speed_floor = 0.01
LANES = 128
SUBL = 8


def shifted(shard, axis, by):
    devices = lax.axis_size(axis)
    pairs = [(i, i + by) for i in range(devices) if 0 <= i + by < devices]
    return lax.ppermute(shard, axis, pairs)


def widen(field, halo, wide):
    cols = field.shape[-1]
    east = shifted(field[..., :halo], "gy", -1)
    west = shifted(field[..., cols - halo :], "gy", 1)
    gap = jnp.zeros(field.shape[:-1] + (wide - cols - 2 * halo,), field.dtype)
    field = jnp.concatenate([field, east, gap, west], axis=-1)
    rows = field.shape[-2]
    south = shifted(field[..., :halo, :], "gx", -1)
    north = shifted(field[..., rows - halo :, :], "gx", 1)
    return jnp.concatenate([north, field, south], axis=-2)


def source_kernel(blocks_ref, recv_ref, wet_ref, out_ref, *, capacity, per_row):
    out_ref[...] = jnp.zeros_like(out_ref)

    def add(s, _):
        b = blocks_ref[s]
        r = pl.multiple_of(b // per_row * SUBL, SUBL)
        c = pl.multiple_of(b % per_row * LANES, LANES)
        here = (pl.ds(r, SUBL), pl.ds(c, LANES))
        out_ref[here] += recv_ref[s // capacity, s % capacity]
        return _

    lax.fori_loop(0, blocks_ref.shape[0], add, 0)
    out_ref[...] = out_ref[...] * wet_ref[...].astype(jnp.float32)


def steps_kernel(
    blocks_ref,
    grow_ref,
    gcol_ref,
    start_ref,
    static_ref,
    gauge_ref,
    recv_ref,
    final_ref,
    adjoint_ref,
    slot_ref,
    read_ref,
    face_ref,
    surf_ref,
    flux_ref,
    coef_ref,
    lam_ref,
    pick_ref,
    *,
    steps,
    halo,
    capacity,
):
    high, wide = start_ref.shape
    rows, cols = final_ref.shape
    strips = high // SUBL
    per_row = cols // LANES
    line = lax.broadcasted_iota(jnp.int32, (SUBL, wide), 0)

    def at(i):
        return pl.ds(pl.multiple_of(i * SUBL, SUBL), SUBL)

    def after(i):
        return at(jnp.minimum(i + 1, strips - 1))

    def east(x):
        return pltpu.roll(x, wide - 1, 1)

    def west(x):
        return pltpu.roll(x, 1, 1)

    def south(x, below):
        return jnp.where(line == SUBL - 1, pltpu.roll(below, SUBL - 1, 0), pltpu.roll(x, SUBL - 1, 0))

    def north(x, above):
        return jnp.where(line == 0, pltpu.roll(above, 1, 0), pltpu.roll(x, 1, 0))

    zero = jnp.zeros((SUBL, wide), jnp.float32)

    def prepare(i, _):
        here, below = at(i), after(i)
        depth, wet, fric = (static_ref[n, here, :] for n in range(3))
        depth_b, wet_b, fric_b = (static_ref[n, below, :] for n in range(3))
        face_ref[0, here, :] = 0.5 * (depth + east(depth))
        face_ref[1, here, :] = wet * east(wet)
        face_ref[2, here, :] = 0.5 * (fric + east(fric))
        face_ref[3, here, :] = 0.5 * (depth + south(depth, depth_b))
        face_ref[4, here, :] = wet * south(wet, wet_b)
        face_ref[5, here, :] = 0.5 * (fric + south(fric, fric_b))
        return _

    lax.fori_loop(0, strips, prepare, 0)

    def face(flux, here, there, depth, wet, rough):
        raw = depth + 0.5 * (here + there)
        total = jnp.maximum(raw, min_depth)
        slope = there - here
        pushed = flux - wave_gain * total * slope
        square = pushed * pushed
        inv_speed = lax.rsqrt(square + speed_floor)
        speed = (square + speed_floor) * inv_speed
        logd = jnp.log(total)
        drag = rough * jnp.exp(logd * (-7.0 / 3.0))
        inv_depth = jnp.exp(-logd)
        ds = drag * speed
        inv = 1.0 / (1.0 + ds)
        wi = wet * inv
        out = wi * pushed
        d_push = wi * (1.0 - drag * square * inv_speed * inv)
        d_total = (7.0 / 3.0) * out * ds * inv * inv_depth - wave_gain * slope * d_push
        half = jnp.where(raw > min_depth, 0.5, jnp.where(raw == min_depth, 0.25, 0.0))
        both = half * d_total
        apart = wave_gain * total * d_push
        return out, d_push, apart + both, both - apart

    for k in range(steps):
        old = start_ref if k == 0 else surf_ref.at[k - 1]

        def forward(i, carry, k=k, old=old):
            cur, flux_above = carry
            here = at(i)
            nxt = old[after(i), :]
            fe = zero if k == 0 else flux_ref[0, here, :]
            fs = zero if k == 0 else flux_ref[1, here, :]
            ne, ae, xe, ye = face(
                fe, cur, east(cur), face_ref[0, here, :], face_ref[1, here, :], face_ref[2, here, :]
            )
            if k:
                coef_ref[k, 0, here, :] = ae
            coef_ref[k, 1, here, :] = xe
            coef_ref[k, 2, here, :] = ye
            ns, a_s, xs, ys = face(
                fs, cur, south(cur, nxt), face_ref[3, here, :], face_ref[4, here, :], face_ref[5, here, :]
            )
            if k:
                coef_ref[k, 3, here, :] = a_s
            coef_ref[k, 4, here, :] = xs
            coef_ref[k, 5, here, :] = ys
            if k < steps - 1:
                flux_ref[0, here, :] = ne
                flux_ref[1, here, :] = ns
            moved = ne - west(ne) + ns - north(ns, flux_above)
            surf_ref[k, here, :] = static_ref[1, here, :] * (cur - mass_gain * moved)
            return nxt, ns

        lax.fori_loop(0, strips, forward, (old[at(0), :], zero))

    final_ref[...] = surf_ref[steps - 1, halo : halo + rows, :cols]
    mine = grow_ref.shape[0]
    lane = lax.broadcasted_iota(jnp.int32, (mine, wide), 1)
    for k in range(steps):
        for g in range(mine):
            pick_ref[pl.ds(g, 1), :] = surf_ref[k, pl.ds(grow_ref[g], 1), :]
        hit = jnp.where(lane == gcol_ref[...], pick_ref[...], 0.0)
        read_ref[k] = jnp.broadcast_to(jnp.sum(hit, axis=1, keepdims=True), read_ref.shape[1:])

    for k in reversed(range(steps)):
        last = k == steps - 1
        src, dst = lam_ref.at[(k + 1) % 2], lam_ref.at[k % 2]

        def seeded(where, k=k, last=last, src=src):
            seed = gauge_ref[0, where, :] * surf_ref[k, where, :] - gauge_ref[1 + k, where, :]
            total = seed if last else src[where, :] + seed
            return static_ref[1, where, :] * total

        def backward(i, carry, k=k, last=last, dst=dst, seeded=seeded):
            cur, above = carry
            here = at(i)
            nxt = seeded(after(i))
            ge = -mass_gain * (cur - east(cur))
            gs = -mass_gain * (cur - south(cur, nxt))
            if not last:
                ge = ge + flux_ref[0, here, :]
                gs = gs + flux_ref[1, here, :]
            if k:
                flux_ref[0, here, :] = ge * coef_ref[k, 0, here, :]
                flux_ref[1, here, :] = gs * coef_ref[k, 3, here, :]
            ve = ge * coef_ref[k, 2, here, :]
            vs = gs * coef_ref[k, 5, here, :]
            dst[here, :] = (
                cur
                + ge * coef_ref[k, 1, here, :]
                + west(ve)
                + gs * coef_ref[k, 4, here, :]
                + north(vs, above)
            )
            return nxt, vs

        lax.fori_loop(0, strips, backward, (seeded(at(0)), zero))

    adjoint_ref[...] = lam_ref[0, halo : halo + rows, :cols]
    lam_ref[1, halo : halo + rows, :cols] = (
        adjoint_ref[...] * static_ref[1, halo : halo + rows, :cols]
    )

    def dots(d, _):
        for j in range(capacity):
            s = d * capacity + j
            b = blocks_ref[s]
            r = pl.multiple_of(b // per_row * SUBL + halo, SUBL)
            c = pl.multiple_of(b % per_row * LANES, LANES)
            prod = lam_ref[1, pl.ds(r, SUBL), pl.ds(c, LANES)] * recv_ref[d, j]
            slot_ref[d, pl.ds(j, 1), :] = jnp.sum(prod, axis=0, keepdims=True)
        return _

    lax.fori_loop(0, recv_ref.shape[0], dots, 0)


def body(
    ocean_depth,
    wet_mask,
    manning,
    fault_slip,
    pattern,
    foot_tile,
    foot_block,
    gauge_row,
    gauge_col,
    observed,
):
    rows, cols = ocean_depth.shape
    steps = observed.shape[0]
    halo = -(-2 * steps // SUBL) * SUBL
    wide = -(-(cols + 2 * halo) // LANES) * LANES
    high = rows + 2 * halo
    width_x = lax.axis_size("gx")
    width_y = lax.axis_size("gy")
    devices = width_x * width_y
    entries = pattern.shape[0]
    per_fault = entries // fault_slip.shape[0]
    capacity = max(2, (2 * entries + devices - 1) // devices)
    per_row = cols // LANES
    f32 = jnp.float32

    target = foot_tile[:, 0]
    order = jnp.arange(entries, dtype=jnp.int32)
    earlier = (target[:, None] == target[None, :]) & (order[:, None] > order[None, :])
    rank = jnp.sum(earlier.astype(jnp.int32), axis=1)
    place = target * capacity + rank
    weights = jnp.repeat(fault_slip, per_fault)
    send_place = target * (capacity + 1) + rank
    is_slot = place[:, None] == jnp.arange(devices * capacity, dtype=jnp.int32)[None, :]
    slot_block = jnp.sum(jnp.where(is_slot, foot_block[:, None], 0), axis=0).astype(f32)
    head = jnp.zeros((devices, SUBL, LANES), f32).at[:, 0, :capacity].set(
        slot_block.reshape(devices, capacity)
    )
    out_rows = (
        jnp.zeros((devices * (capacity + 1), SUBL, LANES), f32)
        .at[send_place]
        .set(pattern * weights[:, None, None])
        .reshape(devices, capacity + 1, SUBL, LANES)
        .at[:, capacity]
        .set(head)
    )
    recv = lax.all_to_all(out_rows, ("gx", "gy"), split_axis=0, concat_axis=0, tiled=True)
    blocks = recv[:, capacity, 0, :capacity].astype(jnp.int32).reshape(-1)

    here_x, here_y = lax.axis_index("gx"), lax.axis_index("gy")
    wet = wet_mask.astype(f32)
    statics = widen(jnp.stack([ocean_depth, wet, manning]), halo, wide)
    local_row = gauge_row - here_x * rows + halo
    local_col = gauge_col - here_y * cols
    local_col = jnp.where(
        (local_col < -halo) | (local_col >= cols + halo), -1, (local_col + wide) % wide
    )
    row_hot = (jnp.arange(high, dtype=jnp.int32)[:, None] == local_row[None, :]).astype(f32)
    col_hot = (local_col[:, None] == jnp.arange(wide, dtype=jnp.int32)[None, :]).astype(f32)
    values = jnp.concatenate([jnp.ones_like(observed[:1]), observed], axis=0)
    gauges = lax.dot_general(
        (values[:, None, :] * row_hot[None]).reshape(-1, values.shape[1]),
        col_hot,
        (((1,), (0,)), ((), ())),
        precision=lax.Precision.HIGHEST,
        preferred_element_type=f32,
    ).reshape(steps + 1, high, wide)
    mine = gauge_row.shape[0] // devices
    me = here_x * width_y + here_y
    my_row = lax.dynamic_slice_in_dim(local_row, me * mine, mine)
    my_col = lax.dynamic_slice_in_dim(local_col, me * mine, mine)

    vmem = pl.BlockSpec(memory_space=pltpu.VMEM)
    smem = pl.BlockSpec(memory_space=pltpu.SMEM)
    params = pltpu.CompilerParams(vmem_limit_bytes=52 * 1024 * 1024)
    start = pl.pallas_call(
        partial(source_kernel, capacity=capacity, per_row=per_row),
        out_shape=jax.ShapeDtypeStruct((rows, cols), f32),
        in_specs=[smem, vmem, vmem],
        out_specs=vmem,
        compiler_params=params,
    )(blocks, recv, wet_mask)
    start = widen(start, halo, wide)
    final_eta, adjoint, per_slot, reads = pl.pallas_call(
        partial(steps_kernel, steps=steps, halo=halo, capacity=capacity),
        out_shape=(
            jax.ShapeDtypeStruct((rows, cols), f32),
            jax.ShapeDtypeStruct((rows, cols), f32),
            jax.ShapeDtypeStruct((devices, capacity, LANES), f32),
            jax.ShapeDtypeStruct((steps, mine, LANES), f32),
        ),
        in_specs=[smem, smem, vmem, vmem, vmem, vmem, vmem],
        out_specs=(vmem, vmem, vmem, vmem),
        scratch_shapes=[
            pltpu.VMEM((6, high, wide), f32),
            pltpu.VMEM((steps, high, wide), f32),
            pltpu.VMEM((2, high, wide), f32),
            pltpu.VMEM((steps, 6, high, wide), f32),
            pltpu.VMEM((2, high, wide), f32),
            pltpu.VMEM((mine, wide), f32),
        ],
        compiler_params=params,
    )(blocks, my_row, my_col[:, None], start, statics, gauges, recv)
    told = jnp.concatenate(
        [
            jnp.sum(per_slot, axis=2),
            jnp.broadcast_to(reads[:, :, 0].reshape(1, -1), (devices, steps * mine)),
        ],
        axis=1,
    )
    heard = lax.all_to_all(told, ("gx", "gy"), split_axis=0, concat_axis=0, tiled=True)
    readings = heard[:, capacity:].reshape(devices, steps, mine)
    readings = readings.transpose(1, 0, 2).reshape(steps, devices * mine)
    per_entry = jnp.sum(jnp.where(is_slot, heard[:, :capacity].reshape(1, -1), 0.0), axis=1)
    grad_slip = jnp.sum(per_entry.reshape(-1, per_fault), axis=1) / fault_slip
    return (final_eta, readings, adjoint, grad_slip)


def solution(mesh):
    placed = (
        P("gx", "gy"),
        P("gx", "gy"),
        P("gx", "gy"),
        P(("gx", "gy")),
        P(("gx", "gy"), None, None),
        P(("gx", "gy"), None),
        P(("gx", "gy")),
        P(),
        P(),
        P(),
    )
    return jax.shard_map(
        body,
        mesh=mesh,
        in_specs=placed,
        out_specs=(P("gx", "gy"), P(), P("gx", "gy"), P(("gx", "gy"))),
        check_vma=False,
    )
```

profile of v0, /device:TPU:0, one launch (start us, length us, event | category | flops | bytes accessed | tf_op | source)
XLA Modules:
  0.0 194.8 jit_solution(3346979285609439598)
XLA Ops:
  0.6 0.9 convert_reduce_fusion
  1.6 0.7 multiply_add_fusion
  2.3 0.8 select_reduce_fusion.1
  3.1 0.7 broadcast_in_dim.67
  4.0 1.6 broadcast_multiply_fusion
  5.5 1.5 broadcast_in_dim.66
  7.1 24.0 %scatter_fusion = f32[544,8,128]{2,1,0:T(8,128)} fusion(f32[544,8,128]{2,1,0:T(8,128)} %broadcast_in_dim.66, s32[256]{0:T(256)S(1)} %bitcast.35, f32[256,8,128]{2,1,0:T(8,128)S(1)} %broadcast_multiply_fusion), kind=kCustom, calls=%fused_computation | custom fusion | bytes 3146752 | tf_op jit(solution)/shard_map/scatter | solution.py:270
  31.1 0.7 pad_dynamic-update-slice_fusion
  31.7 7.2 %all-to-all-start = ((f32[32,17,8,128]{3,2,1,0:T(8,128)}), f32[32,17,8,128]{3,2,1,0:T(8,128)S(1)}, u32[]{:S(2)}, u32[]{:S(2)}) async-start(f32[32,17,8,128]{3,2,1,0:T(8,128)} %pad_dynamic-update-slice_fusion), calls=%async_computation | async-start | bytes 4456448 | tf_op jit(solution)/shard_map/all_to_all | solution.py:275
  39.1 2.1 %pad_maximum_fusion.4 = (f32[3,256,8]{2,1,0:T(8,128)}, f32[3,256,8]{2,1,0:T(8,128)}) fusion(f32[1,256,512]{2,1,0:T(8,128)} %bitcast.21, f32[1,256,512]{2,1,0:T(8,128)S(1)} %convert_bitcast_fusion, f32[1,256,512]{2,1,0:T(8,128)} %bitcast.24), kind=kLoop, calls=%fused_computation.19 | loop fusion | flops 24576 | bytes 1622016 | tf_op jit(solution)/shard_map/slice | solution.py:26
  41.2 1.3 collective-permute-start.4
  42.5 5.3 %collective-permute-start.5 = (f32[3,256,8]{2,1,0:T(8,128)}, f32[3,256,8]{2,1,0:T(8,128)}, u32[]{:S(2)}, u32[]{:S(2)}) collective-permute-start(f32[3,256,8]{2,1,0:T(8,128)} %get-tuple-element.39), channel_id=1, source_target_pairs={{0,1},{1,2},{2,3},{4,5},{5,6},{6,7},{8,9},{9,10},{10,11},{12,13},{... | collective-permute-start | bytes 73736 | tf_op jit(solution)/shard_map/ppermute | solution.py:21
  48.1 5.7 %fusion.gauge_ref = f32[5,272,640]{2,1,0:T(8,128)} fusion(f32[272,512]{1,0:T(8,128)S(1)} %fusion.7, f32[5,512]{1,0:T(8,128)S(1)} %concatenate.26, s32[512]{0:T(512)S(1)} %fusion.10), kind=kOutput, calls=%fused_computation.1 | convolution fusion | flops 5348761600 | bytes 4050944 | tf_op jit(solution)/shard_map/dot_general | solution.py:289
  53.9 35.6 %all-to-all-done.recv_ref = f32[32,17,8,128]{3,2,1,0:T(8,128)S(1)} async-done(((f32[32,17,8,128]{3,2,1,0:T(8,128)}), f32[32,17,8,128]{3,2,1,0:T(8,128)S(1)}, u32[]{:S(2)}, u32[]{:S(2)}) %all-to-all-start) | async-done | bytes 2228256 | tf_op jit(solution)/shard_map/all_to_all | solution.py:275
  89.6 1.2 copy-done.1
  90.9 11.0 %shard_map.129 = f32[256,512]{1,0:T(8,128)S(1)} custom-call(s32[512]{0:T(512)S(1)} %convert_element_type.42.blocks_ref, f32[32,17,8,128]{3,2,1,0:T(8,128)} %copy-done.1, s32[256,512]{1,0:T(8,128)S(1)} %copy-done), custom_call_target="tpu_custom_call" | custom-call | tf_op jit(solution)/shard_map/pallas_call | solution.py:304
  102.0 1.3 collective-permute-start
  103.3 5.6 %collective-permute-start.1 = (f32[256,8]{1,0:T(8,128)S(1)}, f32[256,8]{1,0:T(8,128)S(1)}, u32[]{:S(2)}, u32[]{:S(2)}) collective-permute-start(f32[256,8]{1,0:T(8,128)S(1)} %get-tuple-element.43), channel_id=1, source_target_pairs={{0,1},{1,2},{2,3},{4,5},{5,6},{6,7},{8,9},{9,10},{10,11},{12,13},{... | collective-permute-start | bytes 24584 | tf_op jit(solution)/shard_map/ppermute | solution.py:21
  108.9 0.8 pad_maximum_fusion.10
  109.8 1.7 collective-permute-start.6
  111.5 1.3 collective-permute-start.7
  112.9 3.3 %collective-permute-start.2 = (f32[8,640]{1,0:T(8,128)S(1)}, f32[8,640]{1,0:T(8,128)S(1)}, u32[]{:S(2)}, u32[]{:S(2)}) collective-permute-start(f32[8,640]{1,0:T(8,128)S(1)} %get-tuple-element.40), channel_id=1, source_target_pairs={{0,4},{4,8},{8,12},{12,16},{16,20},{20,24},{24,28},{1,5},{5,9},{9,... | collective-permute-start | bytes 61448 | tf_op jit(solution)/shard_map/ppermute | solution.py:21
  116.2 1.3 collective-permute-start.3
  117.5 2.8 %pad_maximum_fusion.static_ref = f32[3,272,640]{2,1,0:T(8,128)} fusion(f32[3,8,640]{2,1,0:T(8,128)S(1)} %collective-permute-done.7, f32[3,256,8]{2,1,0:T(8,128)} %collective-permute-done.5, f32[3,256,112]{2,1,0:T(8,128)S(1)} %broadcast_in_dim.73, f32[3,256,8]{2,1,0:T(8,128)} %collective-permute-done.4, f32[1,256,512]{2,1,0:T(8,128)S(1)} %bitcast.23, ...), kind=kLoop, calls=%fused_computation.3 | loop fusion | flops 3655680 | bytes 4177920 | tf_op jit(solution)/shard_map/concatenate | solution.py:33
  120.4 0.2 collective-permute-done.3
  120.6 0.1 pad_maximum_fusion.1.start_ref
  120.7 57.3 %shard_map.130 = (f32[256,512]{1,0:T(8,128)}, f32[256,512]{1,0:T(8,128)}, f32[32,16,128]{2,1,0:T(8,128)S(1)}, f32[4,16,128]{2,1,0:T(8,128)S(1)}) custom-call(s32[512]{0:T(512)S(1)} %convert_element_type.42.blocks_ref, s32[16]{0:T(128)S(1)} %dynamic_slice.6.grow_ref, s32[16,1]{1,0:T(8,128)S(1)} %copy.25.gcol_ref, f32[272,640]{1,0:T(8,128)S(1)} %pad_maximum_fusion.1.start_ref, ...), custom_call_target="tpu_custom_call" | custom-call | tf_op jit(solution)/shard_map/pallas_call | solution.py:312
  178.2 0.1 reduce_sum.50
  178.4 14.4 %all_to_all.17 = f32[32,1,80]{2,1,0:T(1,128)S(1)} all-to-all(f32[32,1,80]{2,1,0:T(1,128)S(1)} %bitcast.31), channel_id=1, replica_groups=mesh['gx'=8,'gy'=4] {'gx','gy'}, dimensions={0} | all-to-all | bytes 20480 | tf_op jit(solution)/shard_map/all_to_all | solution.py:339
  193.1 0.2 select_reduce_fusion
  193.5 0.5 div.3
  194.1 0.7 reshape.154
  (51 shorter events, 1.7 us)
Async XLA Ops:
  31.7 7.3 %copy-start = (s32[256,512]{1,0:T(8,128)S(1)}, s32[256,512]{1,0:T(8,128)}, u32[]{:S(2)}) copy-start(s32[256,512]{1,0:T(8,128)} %wet_ref.1) | copy-start | bytes 1572868
  31.7 57.7 %all-to-all-start = ((f32[32,17,8,128]{3,2,1,0:T(8,128)}), f32[32,17,8,128]{3,2,1,0:T(8,128)S(1)}, u32[]{:S(2)}, u32[]{:S(2)}) async-start(f32[32,17,8,128]{3,2,1,0:T(8,128)} %pad_dynamic-update-slice_fusion), calls=%async_computation | async-start | bytes 4456448 | tf_op jit(solution)/shard_map/all_to_all | solution.py:275
  39.0 8.8 %copy-start.5 = (s32[512]{0:T(512)S(1)}, s32[512]{0:T(512)}, u32[]{:S(2)}) copy-start(s32[512]{0:T(512)} %param.21) | copy-start | bytes 6148
  39.0 8.8 %copy-start.6 = (s32[512]{0:T(512)S(1)}, s32[512]{0:T(512)}, u32[]{:S(2)}) copy-start(s32[512]{0:T(512)} %param.22) | copy-start | bytes 6148
  39.0 9.0 %copy-start.4 = (f32[4,512]{1,0:T(4,128)S(1)}, f32[4,512]{1,0:T(4,128)}, u32[]{:S(2)}) copy-start(f32[4,512]{1,0:T(4,128)} %param.23) | copy-start | bytes 24580
  41.2 67.7 %collective-permute-start.4 = (f32[3,256,8]{2,1,0:T(8,128)}, f32[3,256,8]{2,1,0:T(8,128)}, u32[]{:S(2)}, u32[]{:S(2)}) collective-permute-start(f32[3,256,8]{2,1,0:T(8,128)} %get-tuple-element.38), channel_id=1, source_target_pairs={{1,0},{2,1},{3,2},{5,4},{6,5},{7,6},{9,8},{10,9},{11,10},{13,12},{... | collective-permute-start | bytes 73736 | tf_op jit(solution)/shard_map/ppermute | solution.py:21
  42.5 66.4 %collective-permute-start.5 = (f32[3,256,8]{2,1,0:T(8,128)}, f32[3,256,8]{2,1,0:T(8,128)}, u32[]{:S(2)}, u32[]{:S(2)}) collective-permute-start(f32[3,256,8]{2,1,0:T(8,128)} %get-tuple-element.39), channel_id=1, source_target_pairs={{0,1},{1,2},{2,3},{4,5},{5,6},{6,7},{8,9},{9,10},{10,11},{12,13},{... | collective-permute-start | bytes 73736 | tf_op jit(solution)/shard_map/ppermute | solution.py:21
  89.5 1.4 copy-start.1
  90.9 18.0 %copy-start.2 = (f32[256,512]{1,0:T(8,128)S(1)}, f32[256,512]{1,0:T(8,128)}, u32[]{:S(2)}) copy-start(f32[256,512]{1,0:T(8,128)} %param.16) | copy-start | bytes 1572868
  90.9 18.0 %copy-start.3 = (f32[256,512]{1,0:T(8,128)S(1)}, f32[256,512]{1,0:T(8,128)}, u32[]{:S(2)}) copy-start(f32[256,512]{1,0:T(8,128)} %param.14) | copy-start | bytes 1572868
  102.0 10.8 %collective-permute-start = (f32[256,8]{1,0:T(8,128)S(1)}, f32[256,8]{1,0:T(8,128)S(1)}, u32[]{:S(2)}, u32[]{:S(2)}) collective-permute-start(f32[256,8]{1,0:T(8,128)S(1)} %get-tuple-element.42), channel_id=1, source_target_pairs={{1,0},{2,1},{3,2},{5,4},{6,5},{7,6},{9,8},{10,9},{11,10},{13,12},{... | collective-permute-start | bytes 24584 | tf_op jit(solution)/shard_map/ppermute | solution.py:21
  103.3 9.5 %collective-permute-start.1 = (f32[256,8]{1,0:T(8,128)S(1)}, f32[256,8]{1,0:T(8,128)S(1)}, u32[]{:S(2)}, u32[]{:S(2)}) collective-permute-start(f32[256,8]{1,0:T(8,128)S(1)} %get-tuple-element.43), channel_id=1, source_target_pairs={{0,1},{1,2},{2,3},{4,5},{5,6},{6,7},{8,9},{9,10},{10,11},{12,13},{... | collective-permute-start | bytes 24584 | tf_op jit(solution)/shard_map/ppermute | solution.py:21
  109.8 7.8 %collective-permute-start.6 = (f32[3,8,640]{2,1,0:T(8,128)S(1)}, f32[3,8,640]{2,1,0:T(8,128)S(1)}, u32[]{:S(2)}, u32[]{:S(2)}) collective-permute-start(f32[3,8,640]{2,1,0:T(8,128)S(1)} %get-tuple-element.36), channel_id=1, source_target_pairs={{0,4},{4,8},{8,12},{12,16},{16,20},{20,24},{24,28},{1,5},{5,9},{9,... | collective-permute-start | bytes 184328 | tf_op jit(solution)/shard_map/ppermute | solution.py:21
  111.5 6.1 %collective-permute-start.7 = (f32[3,8,640]{2,1,0:T(8,128)S(1)}, f32[3,8,640]{2,1,0:T(8,128)S(1)}, u32[]{:S(2)}, u32[]{:S(2)}) collective-permute-start(f32[3,8,640]{2,1,0:T(8,128)S(1)} %get-tuple-element.37), channel_id=1, source_target_pairs={{4,0},{8,4},{12,8},{16,12},{20,16},{24,20},{28,24},{5,1},{9,5},{13... | collective-permute-start | bytes 184328 | tf_op jit(solution)/shard_map/ppermute | solution.py:21
  112.9 7.5 %collective-permute-start.2 = (f32[8,640]{1,0:T(8,128)S(1)}, f32[8,640]{1,0:T(8,128)S(1)}, u32[]{:S(2)}, u32[]{:S(2)}) collective-permute-start(f32[8,640]{1,0:T(8,128)S(1)} %get-tuple-element.40), channel_id=1, source_target_pairs={{0,4},{4,8},{8,12},{12,16},{16,20},{20,24},{24,28},{1,5},{5,9},{9,... | collective-permute-start | bytes 61448 | tf_op jit(solution)/shard_map/ppermute | solution.py:21
  116.2 4.3 %collective-permute-start.3 = (f32[8,640]{1,0:T(8,128)S(1)}, f32[8,640]{1,0:T(8,128)S(1)}, u32[]{:S(2)}, u32[]{:S(2)}) collective-permute-start(f32[8,640]{1,0:T(8,128)S(1)} %get-tuple-element.41), channel_id=1, source_target_pairs={{4,0},{8,4},{12,8},{16,12},{20,16},{24,20},{28,24},{5,1},{9,5},{13... | collective-permute-start | bytes 61448 | tf_op jit(solution)/shard_map/ppermute | solution.py:21
  120.7 72.8 %copy-start.7 = (f32[16]{0:T(128)S(1)}, f32[16]{0:T(128)}, u32[]{:S(2)}) copy-start(f32[16]{0:T(128)} %param.17) | copy-start | bytes 196
where the time goes:
time: 196 us; the launch traced here: 195 us
  Pallas kernels  68.3 us (35%)
  waiting for transfers between devices  35.8 us (18%)
  local copies, waits for them, and re-layouts  30.2 us (15%)
  starting transfers between devices  28.3 us (14%)
  blocking collectives  14.4 us (7%)
  other arithmetic  11.1 us (6%)
  matrix products  5.73 us (3%)
    pallas_call x1, Pallas kernels, body(): pl.pallas_call(partial(steps_kernel, steps=steps, halo=halo, capacity=cap...  57.3 us
    all_to_all x1, waiting for transfers between devices, body(): lax.all_to_all(out_rows, ('gx', 'gy'), split_axis=0, concat_axis=0, tiled...  35.6 us
    scatter x2, local copies, waits for them, and re-layouts, body(): out_rows = jnp.zeros((devices * (capacity + 1), SUBL, LANES), f32).at[sen...  24.7 us
    ppermute x8, starting transfers between devices, shifted(): return lax.ppermute(shard, axis, pairs)  21.1 us
    all_to_all x1, blocking collectives, body(): lax.all_to_all(told, ('gx', 'gy'), split_axis=0, concat_axis=0, tiled=True)  14.4 us
    pallas_call x1, Pallas kernels, body(): pl.pallas_call(partial(source_kernel, capacity=capacity, per_row=per_row)...  11 us
    all_to_all x1, starting transfers between devices, body(): lax.all_to_all(out_rows, ('gx', 'gy'), split_axis=0, concat_axis=0, tiled...  7.24 us
    dot_general x1, matrix products, body(): lax.dot_general((values[:, None, :] * row_hot[None]).reshape(-1, values.s...  5.73 us
  transfers between devices with their start and end apart: 9, of which 2 were waited for; matrix products, arithmetic and copies ran while one was open for 6% of the time, Pallas kernels for 6%

commit v1 on v0

--- a/solution.py
+++ b/solution.py
@@ -15,37 +15,306 @@
 SUBL = 8
 
 
-def shifted(shard, axis, by):
-    devices = lax.axis_size(axis)
-    pairs = [(i, i + by) for i in range(devices) if 0 <= i + by < devices]
-    return lax.ppermute(shard, axis, pairs)
-
-
-def widen(field, halo, wide):
-    cols = field.shape[-1]
-    east = shifted(field[..., :halo], "gy", -1)
-    west = shifted(field[..., cols - halo :], "gy", 1)
-    gap = jnp.zeros(field.shape[:-1] + (wide - cols - 2 * halo,), field.dtype)
-    field = jnp.concatenate([field, east, gap, west], axis=-1)
-    rows = field.shape[-2]
-    south = shifted(field[..., :halo, :], "gx", -1)
-    north = shifted(field[..., rows - halo :, :], "gx", 1)
-    return jnp.concatenate([north, field, south], axis=-2)
-
-
-def source_kernel(blocks_ref, recv_ref, wet_ref, out_ref, *, capacity, per_row):
-    out_ref[...] = jnp.zeros_like(out_ref)
-
-    def add(s, _):
-        b = blocks_ref[s]
-        r = pl.multiple_of(b // per_row * SUBL, SUBL)
-        c = pl.multiple_of(b % per_row * LANES, LANES)
-        here = (pl.ds(r, SUBL), pl.ds(c, LANES))
-        out_ref[here] += recv_ref[s // capacity, s % capacity]
-        return _
-
-    lax.fori_loop(0, blocks_ref.shape[0], add, 0)
-    out_ref[...] = out_ref[...] * wet_ref[...].astype(jnp.float32)
+def partner_of(number, width_y):
+    return {"gx": number // width_y, "gy": lax.rem(number, width_y)}
+
+
+def greet_all(me, devices, width_y):
+    barrier = pltpu.get_barrier_semaphore()
+
+    def greet(o, _):
+        other = partner_of(lax.rem(me + o, devices), width_y)
+        pl.semaphore_signal(barrier, inc=1, device_id=other, device_id_type=pl.DeviceIdType.MESH)
+        return _
+
+    lax.fori_loop(1, devices, greet, 0)
+    pl.semaphore_wait(barrier, devices - 1)
+
+
+def pack(x, first, halo):
+    parts = LANES // halo
+    per = x.shape[0] // parts
+    group = lax.broadcasted_iota(jnp.int32, (per, LANES), 1) // halo
+    out = jnp.zeros((per, LANES), x.dtype)
+    for c in range(parts):
+        by = (c * halo - first) % LANES
+        part = x[c * per : (c + 1) * per]
+        out = jnp.where(group == c, pltpu.roll(part, by, 1) if by else part, out)
+    return out
+
+
+def unpack(x, first, halo):
+    lane = lax.broadcasted_iota(jnp.int32, x.shape, 1)
+    inside = (lane >= first) & (lane < first + halo)
+    out = []
+    for c in range(LANES // halo):
+        by = (first - c * halo) % LANES
+        out.append(jnp.where(inside, pltpu.roll(x, by, 1) if by else x, 0.0))
+    return jnp.concatenate(out, axis=0)
+
+
+class Rim:
+    def __init__(self, ext_ref, out_buf, in_buf, send_sem, recv_sem, rows, cols, halo):
+        self.ext, self.out, self.inn = ext_ref, out_buf, in_buf
+        self.rows, self.cols, self.halo = rows, cols, halo
+        x, y = lax.axis_index("gx"), lax.axis_index("gy")
+        self.has = (
+            y > 0,
+            y < lax.axis_size("gy") - 1,
+            x > 0,
+            x < lax.axis_size("gx") - 1,
+        )
+        self.to = ({"gy": y - 1}, {"gy": y + 1}, {"gx": x - 1}, {"gx": x + 1})
+        low, end = halo, halo + rows
+        ends = (
+            (out_buf.at[0], in_buf.at[1]),
+            (out_buf.at[1], in_buf.at[0]),
+            (ext_ref.at[:, low : low + halo, :], ext_ref.at[:, end : end + halo, :]),
+            (ext_ref.at[:, end - halo : end, :], ext_ref.at[:, 0:halo, :]),
+        )
+        back = (1, 0, 3, 2)
+        self.copies = [
+            pltpu.make_async_remote_copy(
+                src_ref=ends[d][0],
+                dst_ref=ends[d][1],
+                send_sem=send_sem.at[d],
+                recv_sem=recv_sem.at[back[d]],
+                device_id=self.to[d],
+                device_id_type=pl.DeviceIdType.MESH,
+            )
+            for d in range(4)
+        ]
+        self.back = back
+
+    def greet(self):
+        barrier = pltpu.get_barrier_semaphore()
+        for has, to in zip(self.has, self.to):
+
+            @pl.when(has)
+            def _(to=to):
+                pl.semaphore_signal(
+                    barrier, inc=1, device_id=to, device_id_type=pl.DeviceIdType.MESH
+                )
+
+        pl.semaphore_wait(barrier, sum(has.astype(jnp.int32) for has in self.has))
+
+    def pack_columns(self):
+        inner = slice(self.halo, self.halo + self.rows)
+        for f in range(self.ext.shape[0]):
+            self.out[0, f] = pack(self.ext[f, inner, :LANES], 0, self.halo)
+            self.out[1, f] = pack(
+                self.ext[f, inner, self.cols - LANES : self.cols], LANES - self.halo, self.halo
+            )
+
+    def start(self, d):
+        @pl.when(self.has[d])
+        def _():
+            self.copies[d].start()
+
+    def finish(self, d):
+        @pl.when(self.has[d])
+        def _():
+            self.copies[self.back[d]].wait_recv()
+
+        @pl.when(jnp.logical_not(self.has[d]))
+        def _():
+            if d < 2:
+                self.inn[d] = jnp.zeros(self.inn.shape[1:], jnp.float32)
+            else:
+                at = 0 if d == 2 else self.halo + self.rows
+                self.ext[:, at : at + self.halo, :] = jnp.zeros(
+                    (self.ext.shape[0], self.halo, self.ext.shape[2]), jnp.float32
+                )
+
+    def turn(self):
+        self.finish(0)
+        self.finish(1)
+        inner = slice(self.halo, self.halo + self.rows)
+        for f in range(self.ext.shape[0]):
+            self.ext[f, inner, self.cols :] = unpack(self.inn[1, f], 0, self.halo) + unpack(
+                self.inn[0, f], LANES - self.halo, self.halo
+            )
+        self.start(2)
+        self.start(3)
+
+    def end(self):
+        self.finish(2)
+        self.finish(3)
+        for d in range(4):
+
+            @pl.when(self.has[d])
+            def _(d=d):
+                self.copies[d].wait_send()
+
+
+def spread_kernel(
+    row_ref,
+    weight_ref,
+    pattern_ref,
+    head_ref,
+    depth_ref,
+    wet_ref,
+    fric_ref,
+    grow_ref,
+    gcol_ref,
+    value_ref,
+    recv_ref,
+    static_ref,
+    gauge_ref,
+    send_ref,
+    out_buf,
+    in_buf,
+    send_sem,
+    recv_sem,
+    rim_send,
+    rim_recv,
+    *,
+    halo,
+    capacity,
+):
+    rows, cols = depth_ref.shape
+    high, wide = static_ref.shape[1:]
+    width_y = lax.axis_size("gy")
+    devices = lax.axis_size("gx") * width_y
+    me = lax.axis_index("gx") * width_y + lax.axis_index("gy")
+    rim = Rim(static_ref, out_buf, in_buf, rim_send, rim_recv, rows, cols, halo)
+    for f, ref in enumerate((depth_ref, wet_ref, fric_ref)):
+        static_ref[f, halo : halo + rows, :cols] = ref[...].astype(jnp.float32)
+    rim.pack_columns()
+    greet_all(me, devices, width_y)
+    rim.start(0)
+    rim.start(1)
+
+    def fill(dst, p):
+        for j in range(capacity):
+            s = p * (capacity + 1) + j
+            dst[j] = pattern_ref[row_ref[s]] * weight_ref[s]
+        dst[capacity] = head_ref[p]
+
+    def copy(p, origin):
+        return pltpu.make_async_remote_copy(
+            src_ref=send_ref.at[p],
+            dst_ref=recv_ref.at[origin],
+            send_sem=send_sem.at[p],
+            recv_sem=recv_sem.at[origin],
+            device_id=partner_of(p, width_y),
+            device_id_type=pl.DeviceIdType.MESH,
+        )
+
+    def give(o, _):
+        p = lax.rem(me + o, devices)
+        fill(send_ref.at[p], p)
+        copy(p, me).start()
+        return _
+
+    lax.fori_loop(1, devices, give, 0)
+    fill(recv_ref.at[me], me)
+    rim.turn()
+
+    gauges = grow_ref.shape[1]
+    row_hit = lax.broadcasted_iota(jnp.int32, (high, gauges), 0) == grow_ref[...]
+    col_hit = lax.broadcasted_iota(jnp.int32, (wide, gauges), 0) == gcol_ref[...]
+    col_hot = col_hit.astype(jnp.float32).astype(jnp.bfloat16)
+
+    def placed(value):
+        hot = jnp.where(row_hit, value, 0.0).astype(jnp.bfloat16)
+        return lax.dot_general(
+            hot, col_hot, (((1,), (1,)), ((), ())), preferred_element_type=jnp.float32
+        )
+
+    for q in range(gauge_ref.shape[0]):
+        value = value_ref[pl.ds(q, 1), :]
+        top = value.astype(jnp.bfloat16).astype(jnp.float32)
+        mid = (value - top).astype(jnp.bfloat16).astype(jnp.float32)
+        gauge_ref[q] = placed(top) + placed(mid) + placed(value - top - mid)
+
+    rim.end()
+
+    def take(o, _):
+        p = lax.rem(me + o, devices)
+        copy(me, p).wait_recv()
+        return _
+
+    def gone(o, _):
+        copy(lax.rem(me + o, devices), me).wait_send()
+        return _
+
+    lax.fori_loop(1, devices, take, 0)
+    lax.fori_loop(1, devices, gone, 0)
+
+
+def source_kernel(
+    block_ref,
+    recv_ref,
+    wet_ref,
+    ext_ref,
+    tile_ref,
+    out_buf,
+    in_buf,
+    rim_send,
+    rim_recv,
+    *,
+    halo,
+):
+    rows, cols = wet_ref.shape
+    slots = block_ref.shape[1]
+    count = rows * cols // (SUBL * LANES)
+    rim = Rim(ext_ref, out_buf, in_buf, rim_send, rim_recv, rows, cols, halo)
+    rim.greet()
+    hit = lax.broadcasted_iota(jnp.int32, (count, slots), 0) == block_ref[...]
+    hot = hit.astype(jnp.float32).astype(jnp.bfloat16)
+    for i in range(SUBL):
+        part = recv_ref[pl.ds(i, slots, stride=SUBL), :]
+        top = part.astype(jnp.bfloat16)
+        rest = (part - top.astype(jnp.float32)).astype(jnp.bfloat16)
+        both = jnp.dot(
+            hot, jnp.concatenate([top, rest], axis=1), preferred_element_type=jnp.float32
+        )
+        tile_ref[pl.ds(i, count, stride=SUBL), :] = both[:, :LANES] + both[:, LANES:]
+    for c in range(cols // LANES):
+        lanes = slice(c * LANES, (c + 1) * LANES)
+        ext_ref[0, halo : halo + rows, lanes] = tile_ref[c * rows : (c + 1) * rows, :] * wet_ref[
+            :, lanes
+        ].astype(jnp.float32)
+    rim.pack_columns()
+    rim.start(0)
+    rim.start(1)
+    rim.turn()
+    rim.end()
+
+
+def return_kernel(told_ref, heard_ref, send_sem, recv_sem):
+    width_y = lax.axis_size("gy")
+    devices = lax.axis_size("gx") * width_y
+    me = lax.axis_index("gx") * width_y + lax.axis_index("gy")
+    greet_all(me, devices, width_y)
+
+    def copy(p, origin):
+        return pltpu.make_async_remote_copy(
+            src_ref=told_ref.at[p],
+            dst_ref=heard_ref.at[origin],
+            send_sem=send_sem.at[p],
+            recv_sem=recv_sem.at[origin],
+            device_id=partner_of(p, width_y),
+            device_id_type=pl.DeviceIdType.MESH,
+        )
+
+    def give(o, _):
+        copy(lax.rem(me + o, devices), me).start()
+        return _
+
+    def take(o, _):
+        copy(me, lax.rem(me + o, devices)).wait_recv()
+        return _
+
+    def gone(o, _):
+        copy(lax.rem(me + o, devices), me).wait_send()
+        return _
+
+    lax.fori_loop(1, devices, give, 0)
+    heard_ref[me] = told_ref[me]
+    lax.fori_loop(1, devices, take, 0)
+    lax.fori_loop(1, devices, gone, 0)
 
 
 def steps_kernel(
@@ -73,12 +342,13 @@
 ):
     high, wide = start_ref.shape
     rows, cols = final_ref.shape
-    strips = high // SUBL
+    tall = 2 * SUBL if high % (2 * SUBL) == 0 else SUBL
+    strips = high // tall
     per_row = cols // LANES
-    line = lax.broadcasted_iota(jnp.int32, (SUBL, wide), 0)
+    line = lax.broadcasted_iota(jnp.int32, (tall, wide), 0)
 
     def at(i):
-        return pl.ds(pl.multiple_of(i * SUBL, SUBL), SUBL)
+        return pl.ds(pl.multiple_of(i * tall, tall), tall)
 
     def after(i):
         return at(jnp.minimum(i + 1, strips - 1))
@@ -90,12 +360,12 @@
         return pltpu.roll(x, 1, 1)
 
     def south(x, below):
-        return jnp.where(line == SUBL - 1, pltpu.roll(below, SUBL - 1, 0), pltpu.roll(x, SUBL - 1, 0))
+        return jnp.where(line == tall - 1, pltpu.roll(below, tall - 1, 0), pltpu.roll(x, tall - 1, 0))
 
     def north(x, above):
         return jnp.where(line == 0, pltpu.roll(above, 1, 0), pltpu.roll(x, 1, 0))
 
-    zero = jnp.zeros((SUBL, wide), jnp.float32)
+    zero = jnp.zeros((tall, wide), jnp.float32)
 
     def prepare(i, _):
         here, below = at(i), after(i)
@@ -123,7 +393,8 @@
         drag = rough * jnp.exp(logd * (-7.0 / 3.0))
         inv_depth = jnp.exp(-logd)
         ds = drag * speed
-        inv = 1.0 / (1.0 + ds)
+        inv = pl.reciprocal(1.0 + ds, approx=True)
+        inv = inv * (2.0 - (1.0 + ds) * inv)
         wi = wet * inv
         out = wi * pushed
         d_push = wi * (1.0 - drag * square * inv_speed * inv)
@@ -256,43 +527,24 @@
     order = jnp.arange(entries, dtype=jnp.int32)
     earlier = (target[:, None] == target[None, :]) & (order[:, None] > order[None, :])
     rank = jnp.sum(earlier.astype(jnp.int32), axis=1)
-    place = target * capacity + rank
+    place = target * (capacity + 1) + rank
     weights = jnp.repeat(fault_slip, per_fault)
-    send_place = target * (capacity + 1) + rank
-    is_slot = place[:, None] == jnp.arange(devices * capacity, dtype=jnp.int32)[None, :]
+    slots = devices * (capacity + 1)
+    is_slot = place[:, None] == jnp.arange(slots, dtype=jnp.int32)[None, :]
+    slot_row = jnp.sum(jnp.where(is_slot, order[:, None], 0), axis=0)
+    slot_weight = jnp.sum(jnp.where(is_slot, weights[:, None], 0.0), axis=0)
     slot_block = jnp.sum(jnp.where(is_slot, foot_block[:, None], 0), axis=0).astype(f32)
-    head = jnp.zeros((devices, SUBL, LANES), f32).at[:, 0, :capacity].set(
-        slot_block.reshape(devices, capacity)
+    head = jnp.broadcast_to(
+        jnp.pad(slot_block.reshape(devices, 1, capacity + 1), ((0, 0), (0, 0), (0, LANES - capacity - 1))),
+        (devices, SUBL, LANES),
     )
-    out_rows = (
-        jnp.zeros((devices * (capacity + 1), SUBL, LANES), f32)
-        .at[send_place]
-        .set(pattern * weights[:, None, None])
-        .reshape(devices, capacity + 1, SUBL, LANES)
-        .at[:, capacity]
-        .set(head)
-    )
-    recv = lax.all_to_all(out_rows, ("gx", "gy"), split_axis=0, concat_axis=0, tiled=True)
-    blocks = recv[:, capacity, 0, :capacity].astype(jnp.int32).reshape(-1)
-
     here_x, here_y = lax.axis_index("gx"), lax.axis_index("gy")
-    wet = wet_mask.astype(f32)
-    statics = widen(jnp.stack([ocean_depth, wet, manning]), halo, wide)
     local_row = gauge_row - here_x * rows + halo
     local_col = gauge_col - here_y * cols
     local_col = jnp.where(
         (local_col < -halo) | (local_col >= cols + halo), -1, (local_col + wide) % wide
     )
-    row_hot = (jnp.arange(high, dtype=jnp.int32)[:, None] == local_row[None, :]).astype(f32)
-    col_hot = (local_col[:, None] == jnp.arange(wide, dtype=jnp.int32)[None, :]).astype(f32)
     values = jnp.concatenate([jnp.ones_like(observed[:1]), observed], axis=0)
-    gauges = lax.dot_general(
-        (values[:, None, :] * row_hot[None]).reshape(-1, values.shape[1]),
-        col_hot,
-        (((1,), (0,)), ((), ())),
-        precision=lax.Precision.HIGHEST,
-        preferred_element_type=f32,
-    ).reshape(steps + 1, high, wide)
     mine = gauge_row.shape[0] // devices
     me = here_x * width_y + here_y
     my_row = lax.dynamic_slice_in_dim(local_row, me * mine, mine)
@@ -301,14 +553,61 @@
     vmem = pl.BlockSpec(memory_space=pltpu.VMEM)
     smem = pl.BlockSpec(memory_space=pltpu.SMEM)
     params = pltpu.CompilerParams(vmem_limit_bytes=52 * 1024 * 1024)
+
+    def remote(number):
+        return pltpu.CompilerParams(
+            vmem_limit_bytes=48 * 1024 * 1024, collective_id=number, has_side_effects=True
+        )
+
+    strip = rows * halo // LANES
+    four = [pltpu.SemaphoreType.DMA((4,)), pltpu.SemaphoreType.DMA((4,))]
+    every = [pltpu.SemaphoreType.DMA((devices,)), pltpu.SemaphoreType.DMA((devices,))]
+    recv, statics, gauges = pl.pallas_call(
+        partial(spread_kernel, halo=halo, capacity=capacity),
+        out_shape=(
+            jax.ShapeDtypeStruct((devices, capacity + 1, SUBL, LANES), f32),
+            jax.ShapeDtypeStruct((3, high, wide), f32),
+            jax.ShapeDtypeStruct((steps + 1, high, wide), f32),
+        ),
+        in_specs=[smem] * 2 + [vmem] * 8,
+        out_specs=(vmem,) * 3,
+        scratch_shapes=[
+            pltpu.VMEM((devices, capacity + 1, SUBL, LANES), f32),
+            pltpu.VMEM((2, 3, strip, LANES), f32),
+            pltpu.VMEM((2, 3, strip, LANES), f32),
+        ]
+        + every
+        + four,
+        compiler_params=remote(0),
+    )(
+        slot_row,
+        slot_weight,
+        pattern,
+        head,
+        ocean_depth,
+        wet_mask,
+        manning,
+        local_row[None],
+        local_col[None],
+        values,
+    )
+    blocks = recv[:, capacity, 0, : capacity + 1].astype(jnp.int32)
+    number = blocks % per_row * (rows // SUBL) + blocks // per_row
+    number = jnp.where(jnp.arange(capacity + 1)[None, :] < capacity, number, -1)
     start = pl.pallas_call(
-        partial(source_kernel, capacity=capacity, per_row=per_row),
-        out_shape=jax.ShapeDtypeStruct((rows, cols), f32),
-        in_specs=[smem, vmem, vmem],
+        partial(source_kernel, halo=halo),
+        out_shape=jax.ShapeDtypeStruct((1, high, wide), f32),
+        in_specs=[vmem] * 3,
         out_specs=vmem,
-        compiler_params=params,
-    )(blocks, recv, wet_mask)
-    start = widen(start, halo, wide)
+        scratch_shapes=[
+            pltpu.VMEM((rows * cols // LANES, LANES), f32),
+            pltpu.VMEM((2, 1, strip, LANES), f32),
+            pltpu.VMEM((2, 1, strip, LANES), f32),
+        ]
+        + four,
+        compiler_params=remote(1),
+    )(number.reshape(1, slots), recv.reshape(slots * SUBL, LANES), wet_mask)[0]
+    blocks = blocks[:, :capacity].reshape(-1)
     final_eta, adjoint, per_slot, reads = pl.pallas_call(
         partial(steps_kernel, steps=steps, halo=halo, capacity=capacity),
         out_shape=(
@@ -332,14 +631,24 @@
     told = jnp.concatenate(
         [
             jnp.sum(per_slot, axis=2),
+            jnp.zeros((devices, 1), f32),
             jnp.broadcast_to(reads[:, :, 0].reshape(1, -1), (devices, steps * mine)),
         ],
         axis=1,
     )
-    heard = lax.all_to_all(told, ("gx", "gy"), split_axis=0, concat_axis=0, tiled=True)
-    readings = heard[:, capacity:].reshape(devices, steps, mine)
+    told = jnp.pad(told, ((0, 0), (0, -told.shape[1] % LANES)))
+    heard = pl.pallas_call(
+        return_kernel,
+        out_shape=jax.ShapeDtypeStruct((devices, 1, told.shape[1]), f32),
+        in_specs=[vmem],
+        out_specs=vmem,
+        scratch_shapes=every,
+        compiler_params=remote(2),
+    )(told[:, None, :])[:, 0]
+    readings = heard[:, capacity + 1 : capacity + 1 + steps * mine].reshape(devices, steps, mine)
     readings = readings.transpose(1, 0, 2).reshape(steps, devices * mine)
-    per_entry = jnp.sum(jnp.where(is_slot, heard[:, :capacity].reshape(1, -1), 0.0), axis=1)
+    heard = heard[:, : capacity + 1].reshape(1, -1)
+    per_entry = jnp.sum(jnp.where(is_slot, heard, 0.0), axis=1)
     grad_slip = jnp.sum(per_entry.reshape(-1, per_fault), axis=1) / fault_slip
     return (final_eta, readings, adjoint, grad_slip)
 

time: 196 us -> 133 us (0.68)
  Pallas kernels: 68.3 us -> 114 us
  waiting for transfers between devices: 35.8 us -> 0 us
  starting transfers between devices: 28.3 us -> 0 us
  local copies, waits for them, and re-layouts: 30.2 us -> 10.9 us
  blocking collectives: 14.4 us -> 0 us
  matrix products: 5.73 us -> 0 us
  other arithmetic: 11.1 us -> 6.99 us
    pallas_call x1 -> x3, Pallas kernels: 11 us -> 76.8 us  [the longest x1 60.2 us: body(): pl.pallas_call(partial(spread_kernel, halo=halo, capacity=capacity), out_...]
    all_to_all x1 -> x0, waiting for transfers between devices: 35.6 us -> none  [body(): lax.all_to_all(out_rows, ('gx', 'gy'), split_axis=0, concat_axis=0, tiled...]
    scatter x2 -> x0, local copies, waits for them, and re-layouts: 24.7 us -> none  [body(): out_rows = jnp.zeros((devices * (capacity + 1), SUBL, LANES), f32).at[sen...]
    ppermute x8 -> x0, starting transfers between devices: 21.1 us -> none  [shifted(): return lax.ppermute(shard, axis, pairs)]
    pallas_call x1, Pallas kernels: 57.3 us -> 37.4 us  [body(): pl.pallas_call(partial(steps_kernel, steps=steps, halo=halo, capacity=cap...]
    all_to_all x1 -> x0, blocking collectives: 14.4 us -> none  [body(): lax.all_to_all(told, ('gx', 'gy'), split_axis=0, concat_axis=0, tiled=True)]
    all_to_all x1 -> x0, starting transfers between devices: 7.24 us -> none  [body(): lax.all_to_all(out_rows, ('gx', 'gy'), split_axis=0, concat_axis=0, tiled...]
    unnamed x16, local copies, waits for them, and re-layouts: 1.28 us -> 7.29 us
  transfers between devices with their start and end apart: 9 -> 0, of which waited for: 2 -> 0; matrix products, arithmetic and copies ran while one was open for 6% -> 0% of each run, Pallas kernels for 6% -> 0%
where the time goes in v1:
time: 133 us
  Pallas kernels  114 us (86%)
  local copies, waits for them, and re-layouts  10.9 us (8%)
  other arithmetic  6.99 us (5%)
    pallas_call x1, Pallas kernels, body(): pl.pallas_call(partial(spread_kernel, halo=halo, capacity=capacity), out_...  60.2 us
    pallas_call x1, Pallas kernels, body(): pl.pallas_call(partial(steps_kernel, steps=steps, halo=halo, capacity=cap...  37.4 us
    pallas_call x1, Pallas kernels, body(): pl.pallas_call(return_kernel, out_shape=jax.ShapeDtypeStruct((devices, 1,...  11 us
    unnamed x16, local copies, waits for them, and re-layouts  7.29 us
    pallas_call x1, Pallas kernels, body(): pl.pallas_call(partial(source_kernel, halo=halo), out_shape=jax.ShapeDtyp...  5.57 us

profile of v1, /device:TPU:0, one launch (start us, length us, event | category | flops | bytes accessed | tf_op | source)
XLA Modules:
  0.0 132.9 jit_solution(12442018957195570645)
XLA Ops:
  0.6 0.9 convert_reduce_fusion
  1.6 0.7 multiply_add_fusion
  2.3 1.0 select_reduce_fusion.1
  3.2 0.1 convert_element_type.38
  3.4 0.7 subtract_add_fusion
  4.0 0.7 fusion.4
  4.7 0.7 broadcast_in_dim.102
  5.5 0.2 select_reduce_fusion.2.weight_ref
  5.7 0.7 concatenate.6.value_ref
  6.4 1.0 copy-done.1
  7.5 1.2 copy-done.4
  8.7 1.0 copy-done.5
  9.8 1.0 copy-done.6
  10.8 60.2 %shard_map.129 = (f32[32,17,8,128]{3,2,1,0:T(8,128)}, f32[3,272,640]{2,1,0:T(8,128)S(1)}, f32[5,272,640]{2,1,0:T(8,128)}) custom-call(s32[544]{0:T(1024)S(1)} %get-tuple-element.19.row_ref, f32[544]{0:T(1024)S(1)} %select_reduce_fusion.2.weight_ref, f32[256,8,128]{2,1,0:T(8,128)S(1)} %copy-done.4, f32[32,8,128]{2,1,0:T(8,128)S(1)} %broadcast_in_dim.108.head_ref, ...), custom_call_target="tpu_custom_call" | custom-call | tf_op jit(solution)/shard_map/pallas_call | solution.py:565
  71.0 1.3 copy-done.3
  72.4 1.0 fusion.5
  73.3 0.1 convert_element_type.41
  73.4 0.1 broadcast_in_dim.114
  73.6 1.6 %copy-done = f32[32,17,8,128]{3,2,1,0:T(8,128)S(1)} copy-done((f32[32,17,8,128]{3,2,1,0:T(8,128)S(1)}, f32[32,17,8,128]{3,2,1,0:T(8,128)}, u32[]{:S(2)}) %copy-start) | copy-done | bytes 2228248
  75.2 5.6 %shard_map.130 = f32[1,272,640]{2,1,0:T(8,128)S(1)} custom-call(s32[1,544]{1,0:T(1,128)S(1)} %fusion.3.block_ref, f32[4352,128]{1,0:T(8,128)S(1)} %bitcast.20, s32[256,512]{1,0:T(8,128)S(1)} %copy-done.2), custom_call_target="tpu_custom_call" | custom-call | tf_op jit(solution)/shard_map/pallas_call | solution.py:597
  80.9 0.1 copy.19.gcol_ref
  81.1 0.9 slice_convert_fusion
  82.1 37.4 %shard_map.131 = (f32[256,512]{1,0:T(8,128)}, f32[256,512]{1,0:T(8,128)}, f32[32,16,128]{2,1,0:T(8,128)S(1)}, f32[4,16,128]{2,1,0:T(8,128)S(1)}) custom-call(s32[512]{0:T(512)S(1)} %reshape.142.blocks_ref, s32[16]{0:T(128)S(1)} %dynamic_slice.6.grow_ref, s32[16,1]{1,0:T(8,128)S(1)} %copy.19.gcol_ref, f32[272,640]{1,0:T(8,128)S(1)} %bitcast.21, ...), custom_call_target="tpu_custom_call" | custom-call | tf_op jit(solution)/shard_map/pallas_call | solution.py:611
  119.4 0.1 reduce_sum.70
  119.6 0.1 slice_reduce_fusion
  119.7 0.1 reshape.155
  119.9 11.0 %shard_map.132 = f32[32,1,128]{2,1,0:T(1,128)S(1)} custom-call(f32[32,1,128]{2,1,0:T(1,128)S(1)} %bitcast.24), custom_call_target="tpu_custom_call" | custom-call | tf_op jit(solution)/shard_map/pallas_call | solution.py:640
  131.2 0.7 reshape.145
  131.9 0.1 broadcast_in_dim.119
  132.0 0.2 select_reduce_fusion
  132.2 0.1 reduce_sum.72
  132.3 0.5 div.19
  (28 shorter events, 0.9 us)
Async XLA Ops:
  6.4 1.0 copy-start.1
  7.5 1.2 copy-start.4
  8.7 1.0 copy-start.5
  9.8 1.0 copy-start.6
  10.8 62.8 %copy-start.2 = (s32[256,512]{1,0:T(8,128)S(1)}, s32[256,512]{1,0:T(8,128)}, u32[]{:S(2)}) copy-start(s32[256,512]{1,0:T(8,128)} %wet_ref.3) | copy-start | bytes 1572868
  71.0 1.3 copy-start.3
  73.6 1.6 %copy-start = (f32[32,17,8,128]{3,2,1,0:T(8,128)S(1)}, f32[32,17,8,128]{3,2,1,0:T(8,128)}, u32[]{:S(2)}) copy-start(f32[32,17,8,128]{3,2,1,0:T(8,128)} %get-tuple-element.11.recv_ref) | copy-start | bytes 6684676
  82.1 50.3 %copy-start.7 = (f32[16]{0:T(128)S(1)}, f32[16]{0:T(128)}, u32[]{:S(2)}) copy-start(f32[16]{0:T(128)} %param.13) | copy-start | bytes 196

commit v2 on v1

--- a/solution.py
+++ b/solution.py
@@ -13,6 +13,7 @@
 speed_floor = 0.01
 LANES = 128
 SUBL = 8
+LIMIT = 60 * 1024 * 1024
 
 
 def partner_of(number, width_y):
@@ -159,6 +160,7 @@
     gcol_ref,
     value_ref,
     recv_ref,
+    heads_ref,
     static_ref,
     gauge_ref,
     send_ref,
@@ -166,6 +168,8 @@
     in_buf,
     send_sem,
     recv_sem,
+    head_send,
+    head_recv,
     rim_send,
     rim_recv,
     *,
@@ -180,16 +184,12 @@
     rim = Rim(static_ref, out_buf, in_buf, rim_send, rim_recv, rows, cols, halo)
     for f, ref in enumerate((depth_ref, wet_ref, fric_ref)):
         static_ref[f, halo : halo + rows, :cols] = ref[...].astype(jnp.float32)
-    rim.pack_columns()
     greet_all(me, devices, width_y)
-    rim.start(0)
-    rim.start(1)
 
     def fill(dst, p):
         for j in range(capacity):
-            s = p * (capacity + 1) + j
+            s = p * capacity + j
             dst[j] = pattern_ref[row_ref[s]] * weight_ref[s]
-        dst[capacity] = head_ref[p]
 
     def copy(p, origin):
         return pltpu.make_async_remote_copy(
@@ -201,14 +201,31 @@
             device_id_type=pl.DeviceIdType.MESH,
         )
 
+    def copy_head(p, origin):
+        return pltpu.make_async_remote_copy(
+            src_ref=head_ref.at[p],
+            dst_ref=heads_ref.at[origin],
+            send_sem=head_send.at[p],
+            recv_sem=head_recv.at[origin],
+            device_id=partner_of(p, width_y),
+            device_id_type=pl.DeviceIdType.MESH,
+        )
+
     def give(o, _):
         p = lax.rem(me + o, devices)
         fill(send_ref.at[p], p)
         copy(p, me).start()
-        return _
-
-    lax.fori_loop(1, devices, give, 0)
+        copy_head(p, me).start()
+        return _
+
+    early = min(5, devices)
+    lax.fori_loop(1, early, give, 0)
+    rim.pack_columns()
+    rim.start(0)
+    rim.start(1)
+    lax.fori_loop(early, devices, give, 0)
     fill(recv_ref.at[me], me)
+    heads_ref[me] = head_ref[me]
     rim.turn()
 
     gauges = grow_ref.shape[1]
@@ -233,10 +250,13 @@
     def take(o, _):
         p = lax.rem(me + o, devices)
         copy(me, p).wait_recv()
+        copy_head(me, p).wait_recv()
         return _
 
     def gone(o, _):
-        copy(lax.rem(me + o, devices), me).wait_send()
+        p = lax.rem(me + o, devices)
+        copy(p, me).wait_send()
+        copy_head(p, me).wait_send()
         return _
 
     lax.fori_loop(1, devices, take, 0)
@@ -381,6 +401,11 @@
 
     lax.fori_loop(0, strips, prepare, 0)
 
+    def sweep(work, carry):
+        carry = lax.fori_loop(0, strips // 2, lambda j, c: work(2 * j + 1, work(2 * j, c)), carry)
+        if strips % 2:
+            work(strips - 1, carry)
+
     def face(flux, here, there, depth, wet, rough):
         raw = depth + 0.5 * (here + there)
         total = jnp.maximum(raw, min_depth)
@@ -434,7 +459,7 @@
             surf_ref[k, here, :] = static_ref[1, here, :] * (cur - mass_gain * moved)
             return nxt, ns
 
-        lax.fori_loop(0, strips, forward, (old[at(0), :], zero))
+        sweep(forward, (old[at(0), :], zero))
 
     final_ref[...] = surf_ref[steps - 1, halo : halo + rows, :cols]
     mine = grow_ref.shape[0]
@@ -477,7 +502,7 @@
             )
             return nxt, vs
 
-        lax.fori_loop(0, strips, backward, (seeded(at(0)), zero))
+        sweep(backward, (seeded(at(0)), zero))
 
     adjoint_ref[...] = lam_ref[0, halo : halo + rows, :cols]
     lam_ref[1, halo : halo + rows, :cols] = (
@@ -527,17 +552,14 @@
     order = jnp.arange(entries, dtype=jnp.int32)
     earlier = (target[:, None] == target[None, :]) & (order[:, None] > order[None, :])
     rank = jnp.sum(earlier.astype(jnp.int32), axis=1)
-    place = target * (capacity + 1) + rank
+    place = target * capacity + rank
     weights = jnp.repeat(fault_slip, per_fault)
-    slots = devices * (capacity + 1)
+    slots = devices * capacity
     is_slot = place[:, None] == jnp.arange(slots, dtype=jnp.int32)[None, :]
     slot_row = jnp.sum(jnp.where(is_slot, order[:, None], 0), axis=0)
     slot_weight = jnp.sum(jnp.where(is_slot, weights[:, None], 0.0), axis=0)
     slot_block = jnp.sum(jnp.where(is_slot, foot_block[:, None], 0), axis=0).astype(f32)
-    head = jnp.broadcast_to(
-        jnp.pad(slot_block.reshape(devices, 1, capacity + 1), ((0, 0), (0, 0), (0, LANES - capacity - 1))),
-        (devices, SUBL, LANES),
-    )
+    head = jnp.pad(slot_block.reshape(devices, 1, capacity), ((0, 0), (0, 0), (0, LANES - capacity)))
     here_x, here_y = lax.axis_index("gx"), lax.axis_index("gy")
     local_row = gauge_row - here_x * rows + halo
     local_col = gauge_col - here_y * cols
@@ -552,31 +574,32 @@
 
     vmem = pl.BlockSpec(memory_space=pltpu.VMEM)
     smem = pl.BlockSpec(memory_space=pltpu.SMEM)
-    params = pltpu.CompilerParams(vmem_limit_bytes=52 * 1024 * 1024)
+    params = pltpu.CompilerParams(vmem_limit_bytes=LIMIT)
 
     def remote(number):
         return pltpu.CompilerParams(
-            vmem_limit_bytes=48 * 1024 * 1024, collective_id=number, has_side_effects=True
+            vmem_limit_bytes=LIMIT, collective_id=number, has_side_effects=True
         )
 
     strip = rows * halo // LANES
     four = [pltpu.SemaphoreType.DMA((4,)), pltpu.SemaphoreType.DMA((4,))]
     every = [pltpu.SemaphoreType.DMA((devices,)), pltpu.SemaphoreType.DMA((devices,))]
-    recv, statics, gauges = pl.pallas_call(
+    recv, heads, statics, gauges = pl.pallas_call(
         partial(spread_kernel, halo=halo, capacity=capacity),
         out_shape=(
-            jax.ShapeDtypeStruct((devices, capacity + 1, SUBL, LANES), f32),
+            jax.ShapeDtypeStruct((devices, capacity, SUBL, LANES), f32),
+            jax.ShapeDtypeStruct((devices, 1, LANES), f32),
             jax.ShapeDtypeStruct((3, high, wide), f32),
             jax.ShapeDtypeStruct((steps + 1, high, wide), f32),
         ),
         in_specs=[smem] * 2 + [vmem] * 8,
-        out_specs=(vmem,) * 3,
+        out_specs=(vmem,) * 4,
         scratch_shapes=[
-            pltpu.VMEM((devices, capacity + 1, SUBL, LANES), f32),
+            pltpu.VMEM((devices, capacity, SUBL, LANES), f32),
             pltpu.VMEM((2, 3, strip, LANES), f32),
             pltpu.VMEM((2, 3, strip, LANES), f32),
         ]
-        + every
+        + every * 2
         + four,
         compiler_params=remote(0),
     )(
@@ -591,9 +614,8 @@
         local_col[None],
         values,
     )
-    blocks = recv[:, capacity, 0, : capacity + 1].astype(jnp.int32)
+    blocks = heads[:, 0, :capacity].astype(jnp.int32)
     number = blocks % per_row * (rows // SUBL) + blocks // per_row
-    number = jnp.where(jnp.arange(capacity + 1)[None, :] < capacity, number, -1)
     start = pl.pallas_call(
         partial(source_kernel, halo=halo),
         out_shape=jax.ShapeDtypeStruct((1, high, wide), f32),
@@ -607,7 +629,7 @@
         + four,
         compiler_params=remote(1),
     )(number.reshape(1, slots), recv.reshape(slots * SUBL, LANES), wet_mask)[0]
-    blocks = blocks[:, :capacity].reshape(-1)
+    blocks = blocks.reshape(-1)
     final_eta, adjoint, per_slot, reads = pl.pallas_call(
         partial(steps_kernel, steps=steps, halo=halo, capacity=capacity),
         out_shape=(
@@ -631,7 +653,6 @@
     told = jnp.concatenate(
         [
             jnp.sum(per_slot, axis=2),
-            jnp.zeros((devices, 1), f32),
             jnp.broadcast_to(reads[:, :, 0].reshape(1, -1), (devices, steps * mine)),
         ],
         axis=1,
@@ -645,9 +666,9 @@
         scratch_shapes=every,
         compiler_params=remote(2),
     )(told[:, None, :])[:, 0]
-    readings = heard[:, capacity + 1 : capacity + 1 + steps * mine].reshape(devices, steps, mine)
+    readings = heard[:, capacity : capacity + steps * mine].reshape(devices, steps, mine)
     readings = readings.transpose(1, 0, 2).reshape(steps, devices * mine)
-    heard = heard[:, : capacity + 1].reshape(1, -1)
+    heard = heard[:, :capacity].reshape(1, -1)
     per_entry = jnp.sum(jnp.where(is_slot, heard, 0.0), axis=1)
     grad_slip = jnp.sum(per_entry.reshape(-1, per_fault), axis=1) / fault_slip
     return (final_eta, readings, adjoint, grad_slip)

time: 133 us -> 130 us (0.977)
  Pallas kernels: 114 us -> 110 us
  other arithmetic: 6.99 us -> 9.23 us
  local copies, waits for them, and re-layouts: 10.9 us -> 9.04 us
    unnamed x16 -> x6, local copies, waits for them, and re-layouts: 7.29 us -> 0.01 us
    pallas_call x1, Pallas kernels: 37.4 us -> 30.3 us  [body(): pl.pallas_call(partial(steps_kernel, steps=steps, halo=halo, capacity=cap...]
    pallas_call x1, Pallas kernels: 5.57 us -> 7.92 us  [body(): pl.pallas_call(partial(source_kernel, halo=halo), out_shape=jax.ShapeDtyp...]
where the time goes in v2:
time: 130 us; the launch traced here: 129 us
  Pallas kernels  110 us (85%)
  other arithmetic  9.23 us (7%)
  local copies, waits for them, and re-layouts  9.04 us (7%)
    pallas_call x1, Pallas kernels, body(): pl.pallas_call(partial(spread_kernel, halo=halo, capacity=capacity), out_...  59.9 us
    pallas_call x1, Pallas kernels, body(): pl.pallas_call(partial(steps_kernel, steps=steps, halo=halo, capacity=cap...  30.3 us
    pallas_call x1, Pallas kernels, body(): pl.pallas_call(return_kernel, out_shape=jax.ShapeDtypeStruct((devices, 1,...  12.3 us
    pallas_call x1, Pallas kernels, body(): pl.pallas_call(partial(source_kernel, halo=halo), out_shape=jax.ShapeDtyp...  7.92 us

profile of v2, /device:TPU:0, one launch (start us, length us, event | category | flops | bytes accessed | tf_op | source)
XLA Modules:
  0.0 129.5 jit_solution(12611170344177846712)
XLA Ops:
  0.6 0.9 convert_reduce_fusion
  1.6 0.7 multiply_add_fusion
  2.3 0.7 subtract_add_fusion
  2.9 0.6 dynamic_slice.6.grow_ref
  3.5 0.7 fusion.1
  4.3 1.4 %select_reduce_fusion.1 = (s32[512]{0:T(512)S(1)}, s32[512]{0:T(512)}) fusion(s32[256]{0:T(256)} %param.16, s32[256]{0:T(256)S(1)} %bitcast.25), kind=kLoop, calls=%fused_computation.1 | loop fusion | flops 654336 | bytes 6144 | tf_op jit(solution)/shard_map/reduce_sum | solution.py:561
  5.7 0.7 copy.21.gcol_ref
  6.4 0.7 broadcast_in_dim.79
  7.2 0.1 broadcast_in_dim.80
  7.2 0.7 select_reduce_fusion.2.weight_ref
  8.1 0.6 pad.9.head_ref
  8.7 1.3 %concatenate.6.value_ref = f32[5,512]{1,0:T(8,128)} pad(f32[4,512]{1,0:T(4,128)} %param.19, f32[]{:T(128)} %constant.65.clone.1), padding=1_0x0_0 | pad | bytes 18436 | tf_op jit(solution)/shard_map/concatenate | solution.py:569
  10.0 59.9 %shard_map.129 = (f32[32,16,8,128]{3,2,1,0:T(8,128)}, f32[32,1,128]{2,1,0:T(1,128)}, f32[3,272,640]{2,1,0:T(8,128)}, f32[5,272,640]{2,1,0:T(8,128)}) custom-call(s32[512]{0:T(512)} %get-tuple-element.21.row_ref, f32[512]{0:T(512)} %select_reduce_fusion.2.weight_ref, f32[256,8,128]{2,1,0:T(8,128)} %pattern_ref.1, f32[32,1,128]{2,1,0:T(1,128)} %pad.9.head_ref, ...), custom_call_target="tpu_custom_call" | custom-call | tf_op jit(solution)/shard_map/pallas_call | solution.py:587
  69.9 0.8 fusion.4
  70.7 0.7 convert_element_type.41.blocks_ref
  71.3 0.7 slice_convert_fusion
  72.1 0.1 convert_element_type.42
  72.2 0.6 fusion.3.block_ref
  72.8 7.9 %shard_map.130 = f32[1,272,640]{2,1,0:T(8,128)} custom-call(s32[1,512]{1,0:T(1,128)} %fusion.3.block_ref, f32[4096,128]{1,0:T(8,128)} %bitcast.17, s32[256,512]{1,0:T(8,128)} %wet_ref.3), custom_call_target="tpu_custom_call" | custom-call | tf_op jit(solution)/shard_map/pallas_call | solution.py:619
  80.7 30.3 %shard_map.131 = (f32[256,512]{1,0:T(8,128)}, f32[256,512]{1,0:T(8,128)}, f32[32,16,128]{2,1,0:T(8,128)}, f32[4,16,128]{2,1,0:T(8,128)}) custom-call(s32[512]{0:T(512)} %convert_element_type.41.blocks_ref, s32[16]{0:T(128)} %dynamic_slice.6.grow_ref, s32[16,1]{1,0:T(8,128)} %copy.21.gcol_ref, f32[272,640]{1,0:T(8,128)} %bitcast.18, ...), custom_call_target="tpu_custom_call" | custom-call | tf_op jit(solution)/shard_map/pallas_call | solution.py:633
  111.0 0.8 slice_reduce_fusion
  111.9 0.1 reshape.138
  112.0 1.1 reduce_sum.70
  113.2 0.6 pad.10
  113.8 12.3 %shard_map.132 = f32[32,1,128]{2,1,0:T(1,128)} custom-call(f32[32,1,128]{2,1,0:T(1,128)} %bitcast.24), custom_call_target="tpu_custom_call" | custom-call | tf_op jit(solution)/shard_map/pallas_call | solution.py:661
  126.1 0.8 broadcast_in_dim.91
  126.9 0.2 select_reduce_fusion
  127.2 0.1 reduce_sum.72
  127.3 0.5 div.19
  127.8 0.8 slice.16
  128.6 0.1 copy.22
  128.8 0.7 reshape.126
  (13 shorter events, 0.4 us)
Async XLA Ops:
  2.9 7.1 %copy-start = (s32[512]{0:T(512)}, s32[512]{0:T(512)S(1)}, u32[]{:S(2)}) copy-start(s32[512]{0:T(512)S(1)} %subtract_add_fusion) | copy-start | bytes 6148
  4.2 5.8 %copy-start.1 = (s32[512]{0:T(512)}, s32[512]{0:T(512)S(1)}, u32[]{:S(2)}) copy-start(s32[512]{0:T(512)S(1)} %fusion.1) | copy-start | bytes 6148
  80.7 46.6 %copy-start.2 = (f32[16]{0:T(128)S(1)}, f32[16]{0:T(128)}, u32[]{:S(2)}) copy-start(f32[16]{0:T(128)} %param.13) | copy-start | bytes 196

commit v3 on v2

--- a/solution.py
+++ b/solution.py
@@ -402,9 +402,16 @@
     lax.fori_loop(0, strips, prepare, 0)
 
     def sweep(work, carry):
-        carry = lax.fori_loop(0, strips // 2, lambda j, c: work(2 * j + 1, work(2 * j, c)), carry)
-        if strips % 2:
-            work(strips - 1, carry)
+        at_once = 4
+
+        def several(j, c):
+            for n in range(at_once):
+                c = work(at_once * j + n, c)
+            return c
+
+        carry = lax.fori_loop(0, strips // at_once, several, carry)
+        for i in range(strips // at_once * at_once, strips):
+            carry = work(i, carry)
 
     def face(flux, here, there, depth, wet, rough):
         raw = depth + 0.5 * (here + there)

time: 130 us -> 129 us (level)
  no operation moved by 1% of the time
where the time goes in v3:
time: 129 us; the launch traced here: 128 us
  Pallas kernels  109 us (84%)
  other arithmetic  9.23 us (7%)
  local copies, waits for them, and re-layouts  9.04 us (7%)
    pallas_call x1, Pallas kernels, body(): pl.pallas_call(partial(spread_kernel, halo=halo, capacity=capacity), out_...  59.9 us
    pallas_call x1, Pallas kernels, body(): pl.pallas_call(partial(steps_kernel, steps=steps, halo=halo, capacity=cap...  29 us
    pallas_call x1, Pallas kernels, body(): pl.pallas_call(return_kernel, out_shape=jax.ShapeDtypeStruct((devices, 1,...  12.3 us
    pallas_call x1, Pallas kernels, body(): pl.pallas_call(partial(source_kernel, halo=halo), out_shape=jax.ShapeDtyp...  7.92 us

profile of v3, /device:TPU:0, one launch (start us, length us, event | category | flops | bytes accessed | tf_op | source)
XLA Modules:
  0.0 128.2 jit_solution(16072237807222960541)
XLA Ops:
  0.6 0.9 convert_reduce_fusion
  1.6 0.7 multiply_add_fusion
  2.3 0.7 subtract_add_fusion
  2.9 0.6 dynamic_slice.6.grow_ref
  3.5 0.7 fusion.1
  4.3 1.4 %select_reduce_fusion.1 = (s32[512]{0:T(512)S(1)}, s32[512]{0:T(512)}) fusion(s32[256]{0:T(256)} %param.16, s32[256]{0:T(256)S(1)} %bitcast.25), kind=kLoop, calls=%fused_computation.1 | loop fusion | flops 654336 | bytes 6144 | tf_op jit(solution)/shard_map/reduce_sum | solution.py:568
  5.7 0.7 copy.21.gcol_ref
  6.4 0.7 broadcast_in_dim.79
  7.2 0.1 broadcast_in_dim.80
  7.2 0.7 select_reduce_fusion.2.weight_ref
  8.1 0.6 pad.9.head_ref
  8.7 1.3 %concatenate.6.value_ref = f32[5,512]{1,0:T(8,128)} pad(f32[4,512]{1,0:T(4,128)} %param.19, f32[]{:T(128)} %constant.65.clone.1), padding=1_0x0_0 | pad | bytes 18436 | tf_op jit(solution)/shard_map/concatenate | solution.py:576
  10.0 59.9 %shard_map.129 = (f32[32,16,8,128]{3,2,1,0:T(8,128)}, f32[32,1,128]{2,1,0:T(1,128)}, f32[3,272,640]{2,1,0:T(8,128)}, f32[5,272,640]{2,1,0:T(8,128)}) custom-call(s32[512]{0:T(512)} %get-tuple-element.21.row_ref, f32[512]{0:T(512)} %select_reduce_fusion.2.weight_ref, f32[256,8,128]{2,1,0:T(8,128)} %pattern_ref.1, f32[32,1,128]{2,1,0:T(1,128)} %pad.9.head_ref, ...), custom_call_target="tpu_custom_call" | custom-call | tf_op jit(solution)/shard_map/pallas_call | solution.py:594
  69.9 0.8 fusion.4
  70.7 0.7 convert_element_type.41.blocks_ref
  71.3 0.7 slice_convert_fusion
  72.1 0.1 convert_element_type.42
  72.2 0.6 fusion.3.block_ref
  72.8 7.9 %shard_map.130 = f32[1,272,640]{2,1,0:T(8,128)} custom-call(s32[1,512]{1,0:T(1,128)} %fusion.3.block_ref, f32[4096,128]{1,0:T(8,128)} %bitcast.17, s32[256,512]{1,0:T(8,128)} %wet_ref.3), custom_call_target="tpu_custom_call" | custom-call | tf_op jit(solution)/shard_map/pallas_call | solution.py:626
  80.7 29.0 %shard_map.131 = (f32[256,512]{1,0:T(8,128)}, f32[256,512]{1,0:T(8,128)}, f32[32,16,128]{2,1,0:T(8,128)}, f32[4,16,128]{2,1,0:T(8,128)}) custom-call(s32[512]{0:T(512)} %convert_element_type.41.blocks_ref, s32[16]{0:T(128)} %dynamic_slice.6.grow_ref, s32[16,1]{1,0:T(8,128)} %copy.21.gcol_ref, f32[272,640]{1,0:T(8,128)} %bitcast.18, ...), custom_call_target="tpu_custom_call" | custom-call | tf_op jit(solution)/shard_map/pallas_call | solution.py:640
  109.7 0.8 slice_reduce_fusion
  110.6 0.1 reshape.138
  110.7 1.1 reduce_sum.70
  111.9 0.6 pad.10
  112.5 12.3 %shard_map.132 = f32[32,1,128]{2,1,0:T(1,128)} custom-call(f32[32,1,128]{2,1,0:T(1,128)} %bitcast.24), custom_call_target="tpu_custom_call" | custom-call | tf_op jit(solution)/shard_map/pallas_call | solution.py:668
  124.8 0.8 broadcast_in_dim.91
  125.6 0.2 select_reduce_fusion
  125.9 0.1 reduce_sum.72
  126.0 0.5 div.19
  126.5 0.8 slice.16
  127.3 0.1 copy.22
  127.5 0.7 reshape.126
  (13 shorter events, 0.4 us)
Async XLA Ops:
  2.9 7.1 %copy-start = (s32[512]{0:T(512)}, s32[512]{0:T(512)S(1)}, u32[]{:S(2)}) copy-start(s32[512]{0:T(512)S(1)} %subtract_add_fusion) | copy-start | bytes 6148
  4.2 5.8 %copy-start.1 = (s32[512]{0:T(512)}, s32[512]{0:T(512)S(1)}, u32[]{:S(2)}) copy-start(s32[512]{0:T(512)S(1)} %fusion.1) | copy-start | bytes 6148
  80.7 45.3 %copy-start.2 = (f32[16]{0:T(128)S(1)}, f32[16]{0:T(128)}, u32[]{:S(2)}) copy-start(f32[16]{0:T(128)} %param.13) | copy-start | bytes 196
